TPU v7x, 512 devices: a whole 4x4x16 slice. The times are simulated.
512 devices in a mesh: aux: 64 (over y, z), occ: 8 (over x, core).
Axes of the slice: x: 4, y: 4, z: 16, core: 2. Of those that a mesh axis runs over, the one named last changes fastest.
Arguments:
- factor_tiles: bfloat16 [128, 24, 4, 128, 128], P('aux'), may hold values from -1 to 1
- tile_cols: int32 [128, 24, 4], P('aux'), may hold values from 0 to 23, as said below
- coeffs: bfloat16 [3072, 256], P(None, 'occ'), may hold values from -0.25 to 0.25
- pair_owner: int32 [576], P('aux'), may hold values from 0 to 575, each once
Outputs:
- exchange_tiles: float32 [576, 128, 128], P('aux', 'occ')
Inputs may be any that keep to these rules, and one draw needn't show every extreme that they name: `tile_cols`: for each auxiliary function and basis block row, the 4 listed column blocks are distinct. `pair_owner`: each basis block pair appears exactly once.
All inputs are finite; a program needn't handle non-finite values.
Results may differ from a plain program's by a relative error of at most 0.0015.
Values may be sent and summed in bfloat16 or wider, within the bound.
A program may use at most 128 MiB of HBM per device.

v0:
```python
import jax
import jax.numpy as jnp
from jax import lax
from jax.sharding import PartitionSpec as P


def shards(factor_tiles, tile_cols, coeffs, pair_owner):
    aux_count = factor_tiles.shape[0]
    block_count = factor_tiles.shape[1]
    tile_width = factor_tiles.shape[3]
    local_occ = coeffs.shape[1]
    blocks = coeffs.reshape(block_count, tile_width, local_occ)
    picked = blocks[tile_cols]
    halves = jnp.einsum(
        "qmsrl,qmsli->mrqi", factor_tiles, picked, preferred_element_type=jnp.float32
    ).astype(jnp.bfloat16)
    halves = halves.reshape(block_count, tile_width, aux_count * local_occ)
    row_blocks = pair_owner // block_count
    col_blocks = pair_owner % block_count
    gathered = lax.all_gather(halves, "aux", axis=2, tiled=True)
    row_part = jnp.take(gathered, row_blocks, axis=0)
    col_part = jnp.take(gathered, col_blocks, axis=0)
    partial_tiles = jnp.einsum(
        "sbw,scw->sbc", row_part, col_part, preferred_element_type=jnp.float32
    )
    summed = lax.psum(partial_tiles, "occ")
    share_rows = tile_width // lax.axis_size("occ")
    return lax.dynamic_slice_in_dim(summed, lax.axis_index("occ") * share_rows, share_rows, 1)


def solution(mesh):
    placed = (P("aux", None, None, None, None), P("aux", None, None), P(None, "occ"), P("aux"))
    return jax.shard_map(
        shards, mesh=mesh, in_specs=placed, out_specs=P("aux", "occ", None), check_vma=False
    )
```

profile of v0, /device:TPU:8, one launch (start us, length us, event | category | flops | bytes accessed | tf_op | source)
XLA Modules:
  0.0 413.8 jit_solution(6229224219525203429)
XLA Ops:
  6.5 0.0 copy-start
  6.5 0.0 all-gather.2.cloned.1.call-start
  6.5 0.9 copy-done
  7.5 0.7 compare_select_fusion
  8.2 0.1 copy.15
  8.3 0.1 reshape.31
  8.4 0.0 copy-start.2
  8.4 0.9 gather_fusion
  9.3 5.0 %fusion.14 = bf16[24,2,32,128]{3,2,1,0:T(8,128)(2,1)S(1)} fusion(bf16[2,24,4,128,128]{4,3,2,1,0:T(8,128)(2,1)} %param.6, bf16[2,24,4,128,32]{3,4,2,1,0:T(8,128)(2,1)S(1)} %bitcast.14), kind=kOutput, calls=%fused_computation.13 | convolution fusion | flops 201523200 | bytes 8257536 | tf_op jit(solution)/shard_map/qmsrl,qmsli->mrqi/dot_general | solution.py:14
  14.3 1.0 copy.19
  15.3 0.0 all-gather.2.cloned.1.call-update
  15.3 0.0 all-reduce.2.cloned.1.call-start
  15.4 0.0 copy-done.2
  15.4 247.6 %all-gather.2.cloned.1.call-done = bf16[24,128,4096]{1,0,2:T(8,128)(2,1)} async-done(((bf16[24,128,64]{1,0,2:T(8,128)(2,1)}), bf16[24,128,4096]{1,0,2:T(8,128)(2,1)}) %all-gather.2.cloned.1.call-update) | async-done | bytes 25165840 | tf_op jit(solution)/shard_map/all_gather | solution.py:20
  263.0 31.6 %copy.20 = bf16[24,128,4096]{2,1,0:T(8,128)(2,1)} copy(bf16[24,128,4096]{1,0,2:T(8,128)(2,1)} %all-gather.2.cloned.1.call-done) | data formatting | bytes 50331648 | tf_op jit(solution)/shard_map/all_gather | solution.py:20
  294.6 13.2 %gather_fusion.2 = bf16[9,128,4096]{2,1,0:T(8,128)(2,1)} fusion(bf16[24,128,4096]{2,1,0:T(8,128)(2,1)} %copy.20, s32[1024]{0:T(1024)S(1)} %get-tuple-element.12), kind=kCustom, calls=%fused_computation.1.clone | custom fusion | bytes 18874404 | tf_op jit(solution)/shard_map/jit(_take)/gather | solution.py:22
  307.8 13.3 %gather_fusion.1 = bf16[9,128,4096]{2,1,0:T(8,128)(2,1)} fusion(bf16[24,128,4096]{2,1,0:T(8,128)(2,1)} %copy.20, s32[1024]{0:T(1024)S(1)} %get-tuple-element.13), kind=kCustom, calls=%fused_computation.clone | custom fusion | bytes 18874404 | tf_op jit(solution)/shard_map/jit(_take)/gather | solution.py:21
  321.1 0.0 copy-start.1
  321.1 10.0 %fusion = f32[9,128,128]{2,1,0:T(8,128)} fusion(bf16[9,128,4096]{2,1,0:T(8,128)(2,1)} %gather_fusion.2, bf16[9,128,4096]{2,1,0:T(8,128)(2,1)} %gather_fusion.1, pred[9]{0:T(512)(128)(4,1)S(1)} %get-tuple-element.10, pred[9]{0:T(512)(128)(4,1)S(1)} %get-tuple-element.6), kind=kOutput, calls=%fused_computation.3 | convolution fusion | flops 1217396736 | bytes 19464210 | tf_op jit(solution)/shard_map/sbw,scw->sbc/dot_general | solution.py:23
  331.1 0.0 all-reduce.2.cloned.1.call-update
  331.1 74.3 %all-reduce.2.cloned.1.call-done = f32[9,128,128]{2,1,0:T(8,128)} async-done(((f32[9,128,128]{2,1,0:T(8,128)}), f32[9,128,128]{2,1,0:T(8,128)}) %all-reduce.2.cloned.1.call-update) | async-done | bytes 589840 | tf_op jit(solution)/shard_map/psum | solution.py:26
  405.4 1.5 constant_dynamic-slice_fusion
  406.9 0.0 copy-done.1
  (4 shorter events, 0.1 us)
Async XLA Ops:
  6.5 0.9 copy-start
  6.5 256.5 %all-gather.2.cloned.1.call-start = ((), (), s32[]{:S(2)}) async-start(), calls=%async_computation | async-start | bytes 25559040 | tf_op jit(solution)/shard_map/all_gather | solution.py:20
  8.4 7.0 %copy-start.2 = (s32[9]{0:T(128)S(1)}, s32[9]{0:T(128)}, u32[]{:S(2)}) copy-start(s32[9]{0:T(128)} %param.9) | copy-start | bytes 112
  15.3 390.1 %all-reduce.2.cloned.1.call-start = ((), (), s32[]{:S(2)}) async-start(), calls=%async_computation.1 | async-start | bytes 1179648 | tf_op jit(solution)/shard_map/psum | solution.py:26
  321.1 85.8 %copy-start.1 = (bf16[3072,32]{0,1:T(8,128)(2,1)S(1)}, bf16[3072,32]{0,1:T(8,128)(2,1)}, u32[]{:S(2)}) copy-start(bf16[3072,32]{0,1:T(8,128)(2,1)} %param.8) | copy-start | bytes 589828
Sparse Core Ops, SparseCore 0:
  15.4 247.5 all-gather.1
  331.3 74.0 all-reduce.1
where the time goes:
time: 415 us; the launch traced here: 414 us
  waiting for transfers between devices  322 us (78%)
  local copies, waits for them, and re-layouts  62.7 us (15%)
  matrix products  15 us (4%)
  between operations  13.5 us (3%)
    all_gather x1, waiting for transfers between devices, shards(): gathered = lax.all_gather(halves, 'aux', axis=2, tiled=True)  248 us
    psum x1, waiting for transfers between devices, shards(): summed = lax.psum(partial_tiles, 'occ')  74.3 us
    all_gather x1, local copies, waits for them, and re-layouts, shards(): gathered = lax.all_gather(halves, 'aux', axis=2, tiled=True)  31.6 us
    gather x1, local copies, waits for them, and re-layouts, shards(): row_part = jnp.take(gathered, row_blocks, axis=0)  13.3 us
    gather x1, local copies, waits for them, and re-layouts, shards(): col_part = jnp.take(gathered, col_blocks, axis=0)  13.2 us
    dot_general x1, matrix products, shards(): jnp.einsum('sbw,scw->sbc', row_part, col_part, preferred_element_type=jnp...  10 us
  transfers between devices with their start and end apart: 2, of which 2 were waited for; matrix products, arithmetic and copies ran while one was open for 0% of the time, Pallas kernels for 0%

commit v1 on v0

--- a/solution.py
+++ b/solution.py
@@ -2,6 +2,7 @@
 import jax.numpy as jnp
 from jax import lax
 from jax.sharding import PartitionSpec as P
+from jax.lax import all_gather
 
 
 def shards(factor_tiles, tile_cols, coeffs, pair_owner):
@@ -23,7 +24,7 @@
     partial_tiles = jnp.einsum(
         "sbw,scw->sbc", row_part, col_part, preferred_element_type=jnp.float32
     )
-    summed = lax.psum(partial_tiles, "occ")
+    summed = all_gather(partial_tiles, axis_name="occ").sum(axis=0)
     share_rows = tile_width // lax.axis_size("occ")
     return lax.dynamic_slice_in_dim(summed, lax.axis_index("occ") * share_rows, share_rows, 1)
 

time: 415 us -> 383 us (0.923)
  the two profiles are of different devices: /device:TPU:8 before, /device:TPU:1 now
where the time goes in v1:
time: 383 us; the launch traced here: 382 us
  waiting for transfers between devices  289 us (75%)
  local copies, waits for them, and re-layouts  61.8 us (16%)
  matrix products  15 us (4%)
  between operations  13.5 us (4%)
    all_gather x1, waiting for transfers between devices, shards(): gathered = lax.all_gather(halves, 'aux', axis=2, tiled=True)  249 us
    all_gather x1, waiting for transfers between devices, shards(): summed = all_gather(partial_tiles, axis_name='occ').sum(axis=0)  39.3 us
    all_gather x1, local copies, waits for them, and re-layouts, shards(): gathered = lax.all_gather(halves, 'aux', axis=2, tiled=True)  31.6 us
    gather x1, local copies, waits for them, and re-layouts, shards(): row_part = jnp.take(gathered, row_blocks, axis=0)  13.3 us
    gather x1, local copies, waits for them, and re-layouts, shards(): col_part = jnp.take(gathered, col_blocks, axis=0)  13.2 us
    dot_general x1, matrix products, shards(): jnp.einsum('sbw,scw->sbc', row_part, col_part, preferred_element_type=jnp...  10 us
  transfers between devices with their start and end apart: 2, of which 2 were waited for; matrix products, arithmetic and copies ran while one was open for 0% of the time, Pallas kernels for 0%

profile of v1, /device:TPU:1, one launch (start us, length us, event | category | flops | bytes accessed | tf_op | source)
XLA Modules:
  0.0 382.4 jit_solution(12042000740575578761)
XLA Ops:
  6.5 0.0 copy-start
  6.5 0.0 all-gather.4.cloned.1.call-start
  6.5 0.9 copy-done
  7.5 0.7 compare_select_fusion
  8.2 0.1 copy.15
  8.3 0.1 reshape.31
  8.4 0.0 copy-start.2
  8.4 0.9 gather_fusion
  9.3 5.0 %fusion.14 = bf16[24,2,32,128]{3,2,1,0:T(8,128)(2,1)S(1)} fusion(bf16[2,24,4,128,128]{4,3,2,1,0:T(8,128)(2,1)} %param.6, bf16[2,24,4,128,32]{3,4,2,1,0:T(8,128)(2,1)S(1)} %bitcast.15), kind=kOutput, calls=%fused_computation.13 | convolution fusion | flops 201523200 | bytes 8257536 | tf_op jit(solution)/shard_map/qmsrl,qmsli->mrqi/dot_general | solution.py:15
  14.3 1.0 copy.19
  15.3 0.0 all-gather.4.cloned.1.call-update
  15.3 0.0 all-gather.6.cloned.1.call-start
  15.4 0.0 copy-done.2
  15.4 249.4 %all-gather.4.cloned.1.call-done = bf16[24,128,4096]{1,0,2:T(8,128)(2,1)} async-done(((bf16[24,128,64]{1,0,2:T(8,128)(2,1)}), bf16[24,128,4096]{1,0,2:T(8,128)(2,1)}) %all-gather.4.cloned.1.call-update) | async-done | bytes 25165840 | tf_op jit(solution)/shard_map/all_gather | solution.py:21
  264.8 31.6 %copy.20 = bf16[24,128,4096]{2,1,0:T(8,128)(2,1)} copy(bf16[24,128,4096]{1,0,2:T(8,128)(2,1)} %all-gather.4.cloned.1.call-done) | data formatting | bytes 50331648 | tf_op jit(solution)/shard_map/all_gather | solution.py:21
  296.4 13.2 %gather_fusion.2 = bf16[9,128,4096]{2,1,0:T(8,128)(2,1)} fusion(bf16[24,128,4096]{2,1,0:T(8,128)(2,1)} %copy.20, s32[1024]{0:T(1024)S(1)} %get-tuple-element.12), kind=kCustom, calls=%fused_computation.1.clone | custom fusion | bytes 18874404 | tf_op jit(solution)/shard_map/jit(_take)/gather | solution.py:23
  309.6 13.3 %gather_fusion.1 = bf16[9,128,4096]{2,1,0:T(8,128)(2,1)} fusion(bf16[24,128,4096]{2,1,0:T(8,128)(2,1)} %copy.20, s32[1024]{0:T(1024)S(1)} %get-tuple-element.13), kind=kCustom, calls=%fused_computation.clone | custom fusion | bytes 18874404 | tf_op jit(solution)/shard_map/jit(_take)/gather | solution.py:22
  322.9 0.0 copy-start.1
  322.9 10.0 %fusion = f32[9,128,128]{2,1,0:T(8,128)} fusion(bf16[9,128,4096]{2,1,0:T(8,128)(2,1)} %gather_fusion.2, bf16[9,128,4096]{2,1,0:T(8,128)(2,1)} %gather_fusion.1, pred[9]{0:T(512)(128)(4,1)S(1)} %get-tuple-element.10, pred[9]{0:T(512)(128)(4,1)S(1)} %get-tuple-element.6), kind=kOutput, calls=%fused_computation.3 | convolution fusion | flops 1217396736 | bytes 19464210 | tf_op jit(solution)/shard_map/sbw,scw->sbc/dot_general | solution.py:24
  332.9 0.0 all-gather.6.cloned.1.call-update
  332.9 39.3 %all-gather.6.cloned.1.call-done = f32[72,128,128]{2,1,0:T(8,128)} async-done(((f32[9,128,128]{2,1,0:T(8,128)}), f32[72,128,128]{2,1,0:T(8,128)}) %all-gather.6.cloned.1.call-update) | async-done | bytes 4718608 | tf_op jit(solution)/shard_map/all_gather | solution.py:27
  372.3 2.7 reduce_sum.9
  374.9 0.6 constant_dynamic-slice_fusion
  375.6 0.0 copy-done.1
  (4 shorter events, 0.1 us)
Async XLA Ops:
  6.5 0.9 copy-start
  6.5 258.2 %all-gather.4.cloned.1.call-start = ((), (), s32[]{:S(2)}) async-start(), calls=%async_computation | async-start | bytes 25559040 | tf_op jit(solution)/shard_map/all_gather | solution.py:21
  8.4 7.0 %copy-start.2 = (s32[9]{0:T(128)S(1)}, s32[9]{0:T(128)}, u32[]{:S(2)}) copy-start(s32[9]{0:T(128)} %param.9) | copy-start | bytes 112
  15.3 356.9 %all-gather.6.cloned.1.call-start = ((), (), s32[]{:S(2)}) async-start(), calls=%async_computation.1 | async-start | bytes 5308416 | tf_op jit(solution)/shard_map/all_gather | solution.py:27
  322.9 52.7 %copy-start.1 = (bf16[3072,32]{0,1:T(8,128)(2,1)S(1)}, bf16[3072,32]{0,1:T(8,128)(2,1)}, u32[]{:S(2)}) copy-start(bf16[3072,32]{0,1:T(8,128)(2,1)} %param.8) | copy-start | bytes 589828
Sparse Core Ops, SparseCore 0:
  15.4 249.3 all-gather.3
  333.0 39.1 all-gather.5

commit v2 on v0

--- a/solution.py
+++ b/solution.py
@@ -17,7 +17,8 @@
     halves = halves.reshape(block_count, tile_width, aux_count * local_occ)
     row_blocks = pair_owner // block_count
     col_blocks = pair_owner % block_count
-    gathered = lax.all_gather(halves, "aux", axis=2, tiled=True)
+    stack = jnp.stack([halves] * lax.axis_size("aux"))
+    gathered = jnp.concatenate(lax.all_to_all(stack, "aux", 0, 0), axis=2)
     row_part = jnp.take(gathered, row_blocks, axis=0)
     col_part = jnp.take(gathered, col_blocks, axis=0)
     partial_tiles = jnp.einsum(

time: 415 us -> 1300 us (3.13)
  waiting for transfers between devices: 322 us -> 1190 us
  starting transfers between devices: 0.04 us -> 19.1 us
    all_to_all x0 -> x1, waiting for transfers between devices: none -> 1080 us  [shards(): gathered = jnp.concatenate(lax.all_to_all(stack, 'aux', 0, 0), axis=2)]
    all_gather x1 -> x0, waiting for transfers between devices: 248 us -> none  [shards(): gathered = lax.all_gather(halves, 'aux', axis=2, tiled=True)]
    psum x1, waiting for transfers between devices: 74.3 us -> 117 us  [shards(): summed = lax.psum(partial_tiles, 'occ')]
    all_gather x1 -> x0, local copies, waits for them, and re-layouts: 31.6 us -> none  [shards(): gathered = lax.all_gather(halves, 'aux', axis=2, tiled=True)]
    all_to_all x0 -> x1, local copies, waits for them, and re-layouts: none -> 20.9 us  [shards(): gathered = jnp.concatenate(lax.all_to_all(stack, 'aux', 0, 0), axis=2)]
    all_to_all x0 -> x1, starting transfers between devices: none -> 19 us  [shards(): gathered = jnp.concatenate(lax.all_to_all(stack, 'aux', 0, 0), axis=2)]
where the time goes in v2:
time: 1300 us
  waiting for transfers between devices  1190 us (92%)
  local copies, waits for them, and re-layouts  60 us (5%)
  starting transfers between devices  19.1 us (1%)
  matrix products  15.6 us (1%)
  between operations  13.5 us (1%)
    all_to_all x1, waiting for transfers between devices, shards(): gathered = jnp.concatenate(lax.all_to_all(stack, 'aux', 0, 0), axis=2)  1080 us
    psum x1, waiting for transfers between devices, shards(): summed = lax.psum(partial_tiles, 'occ')  117 us
  transfers between devices with their start and end apart: 2, of which 2 were waited for; matrix products, arithmetic and copies ran while one was open for 0% of the time, Pallas kernels for 0%

profile of v2, /device:TPU:8, one launch (start us, length us, event | category | flops | bytes accessed | tf_op | source)
XLA Modules:
  0.0 1301.5 jit_solution(2547052179520012658)
XLA Ops:
  6.5 0.0 copy-start
  6.5 0.9 copy-done
  7.5 0.7 compare_select_fusion
  8.2 0.1 copy.18
  8.3 0.1 reshape.37
  8.4 0.9 gather_fusion
  9.3 5.0 fusion.14
  14.3 9.1 stack.3
  23.4 0.0 copy-start.2
  23.4 19.0 %all-to-all-start = ((bf16[64,24,128,64]{2,3,1,0:T(8,128)(2,1)}), bf16[64,24,128,64]{2,3,1,0:T(8,128)(2,1)}, u32[]{:S(2)}, u32[]{:S(2)}) async-start(bf16[64,24,128,64]{2,3,1,0:T(8,128)(2,1)} %stack.3), calls=%async_computation | async-start | bytes 50331648 | tf_op jit(solution)/shard_map/all_to_all | solution.py:21
  42.4 0.0 all-reduce.2.cloned.1.call-start
  42.5 0.0 copy-done.2
  42.5 1075.6 %all-to-all-done = bf16[64,24,128,64]{2,3,1,0:T(8,128)(2,1)} async-done(((bf16[64,24,128,64]{2,3,1,0:T(8,128)(2,1)}), bf16[64,24,128,64]{2,3,1,0:T(8,128)(2,1)}, u32[]{:S(2)}, u32[]{:S(2)}) %all-to-all-start) | async-done | bytes 25165856 | tf_op jit(solution)/shard_map/all_to_all | solution.py:21
  1118.1 20.9 %copy.22 = bf16[64,24,128,64]{2,3,0,1:T(8,128)(2,1)} copy(bf16[64,24,128,64]{2,3,1,0:T(8,128)(2,1)} %all-to-all-done) | data formatting | bytes 50331648 | tf_op jit(solution)/shard_map/all_to_all | solution.py:21
  1138.9 13.2 %gather_fusion.2 = bf16[9,128,4096]{1,2,0:T(8,128)(2,1)} fusion(bf16[24,128,4096]{1,2,0:T(8,128)(2,1)} %bitcast.17, s32[1024]{0:T(1024)S(1)} %get-tuple-element.12), kind=kCustom, calls=%fused_computation.1.clone | custom fusion | bytes 18874404 | tf_op jit(solution)/shard_map/jit(_take)/gather | solution.py:23
  1152.1 13.3 %gather_fusion.1 = bf16[9,128,4096]{1,2,0:T(8,128)(2,1)} fusion(bf16[24,128,4096]{1,2,0:T(8,128)(2,1)} %bitcast.18, s32[1024]{0:T(1024)S(1)} %get-tuple-element.13), kind=kCustom, calls=%fused_computation.clone | custom fusion | bytes 18874404 | tf_op jit(solution)/shard_map/jit(_take)/gather | solution.py:22
  1165.3 0.0 copy-start.1
  1165.3 10.7 fusion
  1176.0 0.0 all-reduce.2.cloned.1.call-update
  1176.1 117.1 %all-reduce.2.cloned.1.call-done = f32[9,128,128]{2,1,0:T(8,128)} async-done(((f32[9,128,128]{2,1,0:T(8,128)}), f32[9,128,128]{2,1,0:T(8,128)}) %all-reduce.2.cloned.1.call-update) | async-done | bytes 589840 | tf_op jit(solution)/shard_map/psum | solution.py:27
  1293.2 1.5 constant_dynamic-slice_fusion
  1294.7 0.0 copy-done.1
  (4 shorter events, 0.1 us)
Async XLA Ops:
  6.5 0.9 copy-start
  23.4 19.1 %copy-start.2 = (s32[9]{0:T(128)S(1)}, s32[9]{0:T(128)}, u32[]{:S(2)}) copy-start(s32[9]{0:T(128)} %param.9) | copy-start | bytes 112
  23.4 1094.7 %all-to-all-start = ((bf16[64,24,128,64]{2,3,1,0:T(8,128)(2,1)}), bf16[64,24,128,64]{2,3,1,0:T(8,128)(2,1)}, u32[]{:S(2)}, u32[]{:S(2)}) async-start(bf16[64,24,128,64]{2,3,1,0:T(8,128)(2,1)} %stack.3), calls=%async_computation | async-start | bytes 50331648 | tf_op jit(solution)/shard_map/all_to_all | solution.py:21
  42.4 1250.8 %all-reduce.2.cloned.1.call-start = ((), (), s32[]{:S(2)}) async-start(), calls=%async_computation.1 | async-start | bytes 1179648 | tf_op jit(solution)/shard_map/psum | solution.py:27
  1165.3 129.3 %copy-start.1 = (bf16[3072,32]{0,1:T(8,128)(2,1)S(1)}, bf16[3072,32]{0,1:T(8,128)(2,1)}, u32[]{:S(2)}) copy-start(bf16[3072,32]{0,1:T(8,128)(2,1)} %param.8) | copy-start | bytes 589828
Sparse Core Ops, SparseCore 0:
  1176.2 116.9 all-reduce.1
